TPU v7x, 512 devices: a whole 4x8x8 slice. The times are simulated.
512 devices in a mesh: dp: 128 (over x, z_hi, y), pair: 4 (over z_lo, core).
Axes of the slice: x: 4, y: 8, z: 8 (z_hi: 4, z_lo: 2; z = z_hi * 2 + z_lo), core: 2. Of those that a mesh axis runs over, the one named last changes fastest.
Arguments:
- student: bfloat16 [65536, 768], P(('dp', 'pair')), may hold values from -6 to 6
- teacher: bfloat16 [65536, 768], P(('dp', 'pair')), may hold values from -6 to 6
- band_codes: int32 [5], replicated, may hold values from 1 to 8
Outputs:
- block_loss: float32 [128, 4], P('dp', 'pair')
- student_grad: float32 [65536, 768], P(('dp', 'pair'))
Inputs may be any that keep to these rules, and one draw needn't show every extreme that they name: Kernel m spreads over squared distances of about band_codes[m] * 384.
All inputs are finite; a program needn't handle non-finite values.
Results may differ from a plain program's by a relative error of at most 0.0019.
Values may be sent and summed in bfloat16 or wider, within the bound.
A program may use at most 64 MiB of HBM per device.

v0:
```python
import jax
import jax.numpy as jnp
from jax import lax
from jax.sharding import PartitionSpec as P


def passed_along(shard, axis, by):
    count = lax.axis_size(axis)
    return lax.ppermute(shard, axis, [(i, (i + by) % count) for i in range(count)])


def squares(block):
    return jnp.sum(jnp.square(block.astype(jnp.float32)), axis=1)


def kernels(left_rows, right_rows, band_codes):
    width = left_rows.shape[1]
    inner = lax.dot_general(
        left_rows, right_rows, (((1,), (1,)), ((), ())), preferred_element_type=jnp.float32
    )
    dist = squares(left_rows)[:, None] + squares(right_rows)[None, :] - 2.0 * inner
    value = jnp.zeros_like(dist)
    slope = jnp.zeros_like(dist)
    for index in range(band_codes.shape[0]):
        scale = 2.0 / (band_codes[index].astype(jnp.float32) * width)
        term = jnp.exp(-scale * dist)
        value = value + term
        slope = slope + scale * term
    return (value, slope)


def transposed(coeff, rows):
    return lax.dot_general(
        coeff, rows, (((0,), (0,)), ((), ())), preferred_element_type=jnp.float32
    )


def pair_terms(own, other, band_codes):
    own_s, own_t = (own[0], own[1])
    oth_s, oth_t = (other[0], other[1])
    count = own.shape[1]
    width = own.shape[2]
    g_ss, h_ss = kernels(own_s, oth_s, band_codes)
    g_tt, h_tt = kernels(own_t, oth_t, band_codes)
    g_st, h_st = kernels(own_s, oth_t, band_codes)
    g_ts, h_ts = kernels(own_t, oth_s, band_codes)
    loss = jnp.sum(g_ss + g_tt - g_st - g_ts) / count
    factor = 2.0 * width / count
    c_ss = factor * h_ss
    c_st = factor * h_st
    c_ts = factor * h_ts
    e_ss = c_ss.astype(jnp.bfloat16)
    e_st = c_st.astype(jnp.bfloat16)
    e_ts = c_ts.astype(jnp.bfloat16)
    left = (jnp.sum(c_st, axis=1) - jnp.sum(c_ss, axis=1))[:, None] * own_s.astype(jnp.float32)
    left = (
        left
        + jnp.dot(e_ss, oth_s, preferred_element_type=jnp.float32)
        - jnp.dot(e_st, oth_t, preferred_element_type=jnp.float32)
    )
    right = (jnp.sum(c_ts, axis=0) - jnp.sum(c_ss, axis=0))[:, None] * oth_s.astype(jnp.float32)
    right = right + transposed(e_ss, own_s) - transposed(e_ts, own_t)
    return (loss, left, right)


def fetch(block, rounds):
    pieces = [block]
    moving = block
    for offset in range(1, rounds):
        moving = passed_along(moving, "dp", -1)
        pieces.append(moving)
    return pieces


def deliver(parts):
    carried = parts[-1]
    for offset in reversed(range(len(parts) - 1)):
        carried = passed_along(carried, "dp", 1) + parts[offset]
    return carried


def local(student, teacher, band_codes):
    rounds = lax.axis_size("pair")
    place = lax.axis_index("pair")
    own_shard = jnp.stack([student, teacher])
    own_full = lax.all_gather(own_shard, "pair", axis=1, tiled=True)
    pieces = fetch(own_full, rounds)
    other = lax.dynamic_index_in_dim(jnp.stack(pieces), place, 0, keepdims=False)
    loss, left, right = pair_terms(own_full, other, band_codes)
    masked = [jnp.where(place == offset, right, jnp.zeros_like(right)) for offset in range(rounds)]
    total = left + deliver(masked)
    grad = lax.psum_scatter(total, "pair", scatter_dimension=0, tiled=True)
    return (jnp.reshape(loss, (1, 1)), grad)


def solution(mesh):
    return jax.shard_map(
        local,
        mesh=mesh,
        in_specs=(P(("dp", "pair"), None), P(("dp", "pair"), None), P()),
        out_specs=(P("dp", "pair"), P(("dp", "pair"), None)),
        check_vma=False,
    )
```

profile of v0, /device:TPU:57, one launch (start us, length us, event | category | flops | bytes accessed | tf_op | source)
XLA Modules:
  0.0 528.6 jit_solution(7550467634115095981)
XLA Ops:
  7.2 0.0 all-gather.2.cloned.1.call-start
  7.2 1.8 pad_maximum_fusion
  9.0 0.0 all-gather.2.cloned.1.call-update
  9.0 0.0 reduce-scatter.2.cloned.1.call-start
  9.1 36.4 %all-gather.2.cloned.1.call-done = bf16[2,512,768]{2,1,0:T(8,128)(2,1)} async-done(((bf16[2,128,768]{2,1,0:T(8,128)(2,1)}), bf16[2,512,768]{2,1,0:T(8,128)(2,1)}) %all-gather.2.cloned.1.call-update) | async-done | bytes 1572880 | tf_op jit(solution)/shard_map/all_gather | solution.py:86
  45.5 0.0 copy-start
  45.5 3.2 collective-permute-start
  48.7 70.0 %collective-permute-done = bf16[2,512,768]{2,1,0:T(8,128)(2,1)S(1)} collective-permute-done((bf16[2,512,768]{2,1,0:T(8,128)(2,1)}, bf16[2,512,768]{2,1,0:T(8,128)(2,1)S(1)}, u32[]{:S(2)}, u32[]{:S(2)}) %collective-permute-start) | collective-permute-done | bytes 1572896 | tf_op jit(solution)/shard_map/ppermute | solution.py:9
  118.7 0.0 copy-start.4
  118.7 1.9 collective-permute-start.1
  120.6 66.7 %collective-permute-done.1 = bf16[2,512,768]{2,1,0:T(8,128)(2,1)} collective-permute-done((bf16[2,512,768]{2,1,0:T(8,128)(2,1)S(1)}, bf16[2,512,768]{2,1,0:T(8,128)(2,1)}, u32[]{:S(2)}, u32[]{:S(2)}) %collective-permute-start.1) | collective-permute-done | bytes 1572896 | tf_op jit(solution)/shard_map/ppermute | solution.py:9
  187.3 1.9 collective-permute-start.2
  189.2 1.5 fusion.23
  194.0 1.8 multiply_reduce_fusion.1
  195.8 56.7 %collective-permute-done.2 = bf16[2,512,768]{2,1,0:T(8,128)(2,1)} collective-permute-done((bf16[2,512,768]{2,1,0:T(8,128)(2,1)}, bf16[2,512,768]{2,1,0:T(8,128)(2,1)}, u32[]{:S(2)}, u32[]{:S(2)}) %collective-permute-start.2) | collective-permute-done | bytes 1572896 | tf_op jit(solution)/shard_map/ppermute | solution.py:9
  252.5 0.0 copy-done.4
  252.5 0.0 copy-done
  252.5 2.6 fusion.9
  255.1 0.4 multiply_reduce_fusion
  255.5 1.5 fusion.21
  256.9 0.0 copy-start.6
  256.9 2.5 fusion.22
  259.5 0.0 copy-start.2
  259.5 0.8 copy-done.2
  260.3 0.6 fusion.16
  260.9 0.0 copy-done.6
  260.9 3.0 broadcast_select_fusion
  263.9 1.9 collective-permute-start.3
  265.8 41.9 %collective-permute-done.3 = f32[512,768]{1,0:T(8,128)} collective-permute-done((f32[512,768]{1,0:T(8,128)}, f32[512,768]{1,0:T(8,128)}, u32[]{:S(2)}, u32[]{:S(2)}) %collective-permute-start.3) | collective-permute-done | bytes 1572896 | tf_op jit(solution)/shard_map/ppermute | solution.py:9
  307.7 2.7 select_add_fusion.1
  310.5 10.1 %collective-permute-start.4 = (f32[512,768]{1,0:T(8,128)}, f32[512,768]{1,0:T(8,128)}, u32[]{:S(2)}, u32[]{:S(2)}) collective-permute-start(f32[512,768]{1,0:T(8,128)} %select_add_fusion.1), channel_id=1, source_target_pairs={{0,4},{4,8},{8,12},{12,16},{16,20},{20,24},{24,28},{28,32},{32,36}... | collective-permute-start | bytes 4718600 | tf_op jit(solution)/shard_map/ppermute | solution.py:9
  320.6 53.1 %collective-permute-done.4 = f32[512,768]{1,0:T(8,128)} collective-permute-done((f32[512,768]{1,0:T(8,128)}, f32[512,768]{1,0:T(8,128)}, u32[]{:S(2)}, u32[]{:S(2)}) %collective-permute-start.4) | collective-permute-done | bytes 1572896 | tf_op jit(solution)/shard_map/ppermute | solution.py:9
  373.7 3.2 select_add_fusion
  376.9 10.3 %collective-permute-start.5 = (f32[512,768]{1,0:T(8,128)}, f32[512,768]{1,0:T(8,128)}, u32[]{:S(2)}, u32[]{:S(2)}) collective-permute-start(f32[512,768]{1,0:T(8,128)} %select_add_fusion), channel_id=1, source_target_pairs={{0,4},{4,8},{8,12},{12,16},{16,20},{20,24},{24,28},{28,32},{32,36}... | collective-permute-start | bytes 4718600 | tf_op jit(solution)/shard_map/ppermute | solution.py:9
  387.2 0.0 copy-start.3
  387.2 1.6 fusion.20
  388.8 0.0 copy-start.5
  388.8 0.0 copy-start.1
  388.8 0.0 copy-done.3
  388.8 0.6 fusion.17
  389.4 51.4 %collective-permute-done.5 = f32[512,768]{1,0:T(8,128)} collective-permute-done((f32[512,768]{1,0:T(8,128)}, f32[512,768]{1,0:T(8,128)}, u32[]{:S(2)}, u32[]{:S(2)}) %collective-permute-start.5) | collective-permute-done | bytes 1572896 | tf_op jit(solution)/shard_map/ppermute | solution.py:9
  440.8 0.0 copy-done.5
  440.8 0.0 copy-done.1
  440.8 4.1 fusion.3
  444.9 0.0 reduce-scatter.2.cloned.1.call-update
  444.9 5.4 %subtract_reduce_fusion = f32[]{:T(128)} fusion(f32[512,512]{1,0:T(8,128)} %get-tuple-element.14, f32[512,512]{1,0:T(8,128)} %copy-done.5, f32[512,512]{1,0:T(8,128)} %copy-done.6, f32[512]{0:T(512)S(1)} %get-tuple-element.4, f32[512]{0:T(512)S(1)} %get-tuple-element.2, f32[]{:T(128)S(6)} %neg.14, f32[]{:T(128)S(6)} %neg.13, f32[]{:T(128)S(6)} %neg.12, ...), kind=kOutput, calls=%fused_computation.33 | convolution fusion | flops 413925376 | bytes 4722712 | tf_op jit(solution)/shard_map/dot_general | solution.py:18
  451.0 69.6 %reduce-scatter.2.cloned.1.call-done = f32[128,768]{1,0:T(8,128)} async-done(((f32[512,768]{1,0:T(8,128)}), f32[128,768]{1,0:T(8,128)}) %reduce-scatter.2.cloned.1.call-update) | async-done | bytes 393232 | tf_op jit(solution)/shard_map/reduce_scatter | solution.py:92
  (2 shorter events, 0.0 us)
Async XLA Ops:
  7.2 38.3 %all-gather.2.cloned.1.call-start = ((), (), s32[]{:S(2)}) async-start(), calls=%async_computation.1 | async-start | bytes 1966080 | tf_op jit(solution)/shard_map/all_gather | solution.py:86
  9.0 511.6 %reduce-scatter.2.cloned.1.call-start = ((), (), s32[]{:S(2)}) async-start(), calls=%async_computation.2 | async-start | bytes 1966080 | tf_op jit(solution)/shard_map/reduce_scatter | solution.py:92
  45.5 207.1 %copy-start = (bf16[2,512,768]{2,1,0:T(8,128)(2,1)S(1)}, bf16[2,512,768]{2,1,0:T(8,128)(2,1)}, u32[]{:S(2)}) copy-start(bf16[2,512,768]{2,1,0:T(8,128)(2,1)} %all-gather.2.cloned.1.call-done) | copy-start | bytes 4718596
  45.5 73.2 %collective-permute-start = (bf16[2,512,768]{2,1,0:T(8,128)(2,1)}, bf16[2,512,768]{2,1,0:T(8,128)(2,1)S(1)}, u32[]{:S(2)}, u32[]{:S(2)}) collective-permute-start(bf16[2,512,768]{2,1,0:T(8,128)(2,1)} %all-gather.2.cloned.1.call-done), channel_id=1, source_target_pairs={{0,508},{4,0},{8,4},{12,8},{16,12},{20,16},{24,20},{28,24},{32,28}... | collective-permute-start | bytes 4718600 | tf_op jit(solution)/shard_map/ppermute | solution.py:9
  118.7 133.9 %copy-start.4 = (bf16[2,512,768]{2,1,0:T(8,128)(2,1)}, bf16[2,512,768]{2,1,0:T(8,128)(2,1)S(1)}, u32[]{:S(2)}) copy-start(bf16[2,512,768]{2,1,0:T(8,128)(2,1)S(1)} %collective-permute-done) | copy-start | bytes 4718596
  118.7 68.6 %collective-permute-start.1 = (bf16[2,512,768]{2,1,0:T(8,128)(2,1)S(1)}, bf16[2,512,768]{2,1,0:T(8,128)(2,1)}, u32[]{:S(2)}, u32[]{:S(2)}) collective-permute-start(bf16[2,512,768]{2,1,0:T(8,128)(2,1)S(1)} %collective-permute-done), channel_id=1, source_target_pairs={{0,508},{4,0},{8,4},{12,8},{16,12},{20,16},{24,20},{28,24},{32,28}... | collective-permute-start | bytes 4718600 | tf_op jit(solution)/shard_map/ppermute | solution.py:9
  187.3 65.2 %collective-permute-start.2 = (bf16[2,512,768]{2,1,0:T(8,128)(2,1)}, bf16[2,512,768]{2,1,0:T(8,128)(2,1)}, u32[]{:S(2)}, u32[]{:S(2)}) collective-permute-start(bf16[2,512,768]{2,1,0:T(8,128)(2,1)} %collective-permute-done.1), channel_id=1, source_target_pairs={{0,508},{4,0},{8,4},{12,8},{16,12},{20,16},{24,20},{28,24},{32,28}... | collective-permute-start | bytes 4718600 | tf_op jit(solution)/shard_map/ppermute | solution.py:9
  256.9 4.0 copy-start.6
  259.5 0.8 copy-start.2
  263.9 43.8 %collective-permute-start.3 = (f32[512,768]{1,0:T(8,128)}, f32[512,768]{1,0:T(8,128)}, u32[]{:S(2)}, u32[]{:S(2)}) collective-permute-start(f32[512,768]{1,0:T(8,128)} %get-tuple-element.17), channel_id=1, source_target_pairs={{0,4},{4,8},{8,12},{12,16},{16,20},{20,24},{24,28},{28,32},{32,36}... | collective-permute-start | bytes 4718600 | tf_op jit(solution)/shard_map/ppermute | solution.py:9
  310.5 63.2 %collective-permute-start.4 = (f32[512,768]{1,0:T(8,128)}, f32[512,768]{1,0:T(8,128)}, u32[]{:S(2)}, u32[]{:S(2)}) collective-permute-start(f32[512,768]{1,0:T(8,128)} %select_add_fusion.1), channel_id=1, source_target_pairs={{0,4},{4,8},{8,12},{12,16},{16,20},{20,24},{24,28},{28,32},{32,36}... | collective-permute-start | bytes 4718600 | tf_op jit(solution)/shard_map/ppermute | solution.py:9
  376.9 64.0 %collective-permute-start.5 = (f32[512,768]{1,0:T(8,128)}, f32[512,768]{1,0:T(8,128)}, u32[]{:S(2)}, u32[]{:S(2)}) collective-permute-start(f32[512,768]{1,0:T(8,128)} %select_add_fusion), channel_id=1, source_target_pairs={{0,4},{4,8},{8,12},{12,16},{16,20},{20,24},{24,28},{28,32},{32,36}... | collective-permute-start | bytes 4718600 | tf_op jit(solution)/shard_map/ppermute | solution.py:9
  387.2 1.6 copy-start.3
  388.8 52.1 %copy-start.5 = (f32[512,512]{1,0:T(8,128)}, f32[512,512]{1,0:T(8,128)S(1)}, u32[]{:S(2)}) copy-start(f32[512,512]{1,0:T(8,128)S(1)} %get-tuple-element.20) | copy-start | bytes 3145732
  388.8 52.0 %copy-start.1 = (f32[512,768]{1,0:T(8,128)S(1)}, f32[512,768]{1,0:T(8,128)}, u32[]{:S(2)}) copy-start(f32[512,768]{1,0:T(8,128)} %get-tuple-element.18) | copy-start | bytes 4718596
Sparse Core Ops, SparseCore 0:
  10.7 34.7 all-gather.1
  445.0 75.5 reduce-scatter.1
where the time goes:
time: 531 us; the launch traced here: 529 us
  waiting for transfers between devices  446 us (84%)
  starting transfers between devices  29.4 us (6%)
  between operations  19.3 us (4%)
  matrix products  19.2 us (4%)
  other arithmetic  12.5 us (2%)
    ppermute x6, waiting for transfers between devices, passed_along(): lax.ppermute(shard, axis, [(i, (i + by) % count) for i in range(count)])  340 us
    reduce_scatter x1, waiting for transfers between devices, local(): grad = lax.psum_scatter(total, 'pair', scatter_dimension=0, tiled=True)  69.6 us
    all_gather x1, waiting for transfers between devices, local(): own_full = lax.all_gather(own_shard, 'pair', axis=1, tiled=True)  36.4 us
    ppermute x6, starting transfers between devices, passed_along(): lax.ppermute(shard, axis, [(i, (i + by) % count) for i in range(count)])  29.4 us
    dot_general x4, matrix products, kernels(): lax.dot_general(left_rows, right_rows, (((1,), (1,)), ((), ())), preferre...  11 us
  transfers between devices with their start and end apart: 8, of which 8 were waited for; matrix products, arithmetic and copies ran while one was open for 2% of the time, Pallas kernels for 0%

commit v1 on v0

v1 whole, which is shorter than its diff:
```python
import jax
import jax.numpy as jnp
from jax import lax
from jax.experimental import pallas as pl
from jax.experimental.pallas import tpu as pltpu
from jax.sharding import PartitionSpec as P

REACH = 3
LOG2E = 1.4426950408889634


def kernel(student, teacher, codes, loss_out, grad_out,
           bb, cbuf, nb, nc, inner, ebuf, acc, rows_acc, loss_acc, loss_in, got, z_out, z_in,
           local_sem, dp_send, dp_recv, pair_send, pair_recv, fin_send, fin_recv, loss_send, loss_recv):
    n_dp = lax.axis_size("dp")
    part, width = student.shape
    count = 4 * part
    bands = codes.shape[0]
    b = lax.axis_index("dp")
    p = lax.axis_index("pair")
    z_lo = p // 2
    core = p % 2
    sib = z_lo * 2 + (1 - core)
    zp = (1 - z_lo) * 2 + core
    diag = (1 - z_lo) * 2 + (1 - core)
    up = (b + 1) % n_dp
    down = (b + n_dp - 1) % n_dp

    def dev(block, place):
        return {"dp": block, "pair": place}

    def rows_of(q, chunk):
        return pl.ds(pl.multiple_of(chunk * count + q * part, part), part)

    barrier = pltpu.get_barrier_semaphore()
    for target in (dev(up, p), dev(down, p), dev(b, sib), dev(b, zp), dev(b, diag)):
        pl.semaphore_signal(barrier, inc=1, device_id=target, device_id_type=pl.DeviceIdType.MESH)
    pl.semaphore_wait(barrier, 5)

    own = (student, teacher)

    def remote(src, dst, ssem, rsem, target):
        return pltpu.make_async_remote_copy(
            src_ref=src, dst_ref=dst, send_sem=ssem, recv_sem=rsem,
            device_id=target, device_id_type=pl.DeviceIdType.MESH)

    def half(slot, chunk):
        return cbuf.at[slot, pl.ds(chunk * part, part)]

    def dp_copy(way, step, chunk):
        sign = -1 if way == 0 else 1
        src = own[chunk] if step == 1 else half(REACH + sign * (step - 1), chunk)
        dst = half(REACH + sign * step, chunk)
        return remote(src, dst, dp_send.at[way, step - 1, chunk], dp_recv.at[way, step - 1, chunk],
                      dev(up if way == 0 else down, p))

    def pair_copy(rel, chunk):
        if rel == 2:
            src = dst = bb.at[rows_of(zp, chunk)]
        else:
            src, dst = own[chunk], bb.at[rows_of(p, chunk)]
        target = dev(b, zp if rel == 1 else sib)
        return remote(src, dst, pair_send.at[rel, chunk], pair_recv.at[rel, chunk], target)

    def pair_arrived(rel, chunk):
        q = (sib, zp, diag)[rel]
        ref = bb.at[rows_of(q, chunk)]
        remote(ref, ref, pair_send.at[rel, chunk], pair_recv.at[rel, chunk], dev(b, sib)).wait_recv()

    local = [pltpu.make_async_copy(own[c], half(REACH, c), local_sem.at[0, c]) for c in (0, 1)]
    local += [pltpu.make_async_copy(own[c], bb.at[rows_of(p, c)], local_sem.at[1, c]) for c in (0, 1)]
    for chunk in (0, 1):
        for way in (0, 1):
            dp_copy(way, 1, chunk).start()
        pair_copy(1, chunk).start()
    for chunk in (0, 1):
        pair_copy(0, chunk).start()
    for c in local:
        c.start()

    scale = [2.0 / (codes[m].astype(jnp.float32) * width) for m in range(bands)]
    expo = [s * (-LOG2E) for s in scale]
    factor = 2.0 * width / count
    slope = [s * factor for s in scale]

    acc[...] = jnp.zeros_like(acc)
    rows_acc[...] = jnp.zeros_like(rows_acc)
    loss_acc[...] = jnp.zeros_like(loss_acc)

    def split_squares(x):
        sq = jnp.square(x.astype(jnp.float32))
        hi = sq.astype(jnp.bfloat16)
        lo = (sq - hi.astype(jnp.float32)).astype(jnp.bfloat16)
        return hi, lo

    def nt(x, y):
        return lax.dot_general(x, y, (((1,), (1,)), ((), ())), preferred_element_type=jnp.float32)

    def row_norms(q, chunk):
        here = rows_of(q, chunk)
        hi, lo = split_squares(bb[here, :])
        ones = jnp.ones((128, width), jnp.bfloat16)
        nb[here, :] = nt(hi, ones) + nt(lo, ones)

    def col_norms(slot):
        hi, lo = split_squares(cbuf[slot])
        ones = jnp.ones((8, width), jnp.bfloat16)
        nc[slot] = nt(ones, hi) + nt(ones, lo)

    step_rows = 32

    def work(offset):
        slot = REACH + offset
        ahead = offset >= 0
        weight = [2.0 * w for w in slope] if offset == 0 else slope
        col_norms(slot)
        cols = cbuf[slot]
        inner[pl.ds(0, count), :] = nt(bb[pl.ds(0, count), :], cols)
        if ahead:
            inner[pl.ds(count, count), :] = nt(bb[pl.ds(count, count), :], cols)

        def dist(here, at):
            norm = nb[here, :] + nc[slot, 0:1, pl.ds(at * part, part)]
            return norm - 2.0 * inner[here, pl.ds(at * part, part)]

        def sums(d, want_value, want_slope):
            value = slope_sum = None
            for m in range(bands):
                term = jnp.exp2(d * expo[m])
                if want_value:
                    value = term if value is None else value + term
                if want_slope:
                    scaled = term * weight[m]
                    slope_sum = scaled if slope_sum is None else slope_sum + scaled
            return value, slope_sum

        def fold(x):
            return jnp.sum(x.reshape(step_rows // 8, 8, part), axis=0)

        def body(i, total):
            here = pl.ds(pl.multiple_of(i * step_rows, step_rows), step_rows)
            g_ss, c_ss = sums(dist(here, 0), ahead, True)
            g_st, c_st = sums(dist(here, 1), ahead, True)
            ebuf[here, pl.ds(0, part)] = c_ss.astype(jnp.bfloat16)
            ebuf[here, pl.ds(part, part)] = (-c_st).astype(jnp.bfloat16)
            rows_acc[here, :] += c_st - c_ss
            if ahead:
                total = total + fold(g_ss - g_st)
                there = pl.ds(pl.multiple_of(count + i * step_rows, step_rows), step_rows)
                g_ts, _ = sums(dist(there, 0), True, False)
                g_tt, _ = sums(dist(there, 1), True, False)
                total = total + fold(g_tt - g_ts)
            return total

        total = lax.fori_loop(0, count // step_rows, body, jnp.zeros((8, part), jnp.float32))
        if ahead:
            loss_acc[offset] = total
        acc[...] += jnp.dot(ebuf[...], cols, preferred_element_type=jnp.float32)

    def arrived(step, chunk):
        for way in (0, 1):
            dp_copy(way, step, chunk).wait_recv()
            if step < REACH:
                dp_copy(way, step + 1, chunk).start()

    for c in local:
        c.wait()
    for chunk in (0, 1):
        row_norms(p, chunk)
        pair_arrived(0, chunk)
        row_norms(sib, chunk)
    for chunk in (0, 1):
        arrived(1, chunk)
        pair_arrived(1, chunk)
        pair_copy(2, chunk).start()
        row_norms(zp, chunk)
    for chunk in (0, 1):
        pair_arrived(2, chunk)
        row_norms(diag, chunk)
    work(0)
    work(1)
    arrived(2, 0)
    work(-1)
    arrived(2, 1)
    work(2)
    work(-2)
    arrived(3, 0)
    arrived(3, 1)
    work(3)
    work(-3)

    def loss_copy(rel):
        q = (sib, zp, diag)[rel]
        return remote(loss_acc.at[q], loss_in.at[rel], loss_send.at[rel], loss_recv.at[rel], dev(b, q))

    for rel in range(3):
        loss_copy(rel).start()

    def finish(q):
        here = pl.ds(pl.multiple_of(q * part, part), part)
        row = jnp.sum(rows_acc[here, :], axis=1, keepdims=True)
        acc[here, :] += row * bb[here, :].astype(jnp.float32)

    def sib_copy(which):
        q = (diag, sib)[which]
        here = pl.ds(pl.multiple_of(q * part, part), part)
        return remote(acc.at[here], got.at[which], fin_send.at[which], fin_recv.at[which], dev(b, sib))

    finish(diag)
    sib_copy(0).start()
    finish(sib)
    sib_copy(1).start()
    finish(zp)
    finish(p)
    sib_copy(0).wait_recv()
    zrow = pl.ds(pl.multiple_of(zp * part, part), part)
    z_out[...] = acc[zrow, :] + got[0]
    z_copy = remote(z_out, z_in, fin_send.at[2], fin_recv.at[2], dev(b, zp))
    z_copy.start()
    sib_copy(1).wait_recv()
    prow = pl.ds(pl.multiple_of(p * part, part), part)
    mine = acc[prow, :] + got[1]
    for rel in range(3):
        loss_copy(rel).wait_recv()
    total = loss_acc[p] + loss_in[0] + loss_in[1] + loss_in[2]
    loss_out[...] = jnp.sum(jnp.sum(total, axis=1, keepdims=True), axis=0, keepdims=True) * (1.0 / count)
    z_copy.wait_recv()
    grad_out[...] = mine + z_in[...]

    for chunk in (0, 1):
        for way in (0, 1):
            for step in range(1, REACH + 1):
                dp_copy(way, step, chunk).wait_send()
        for rel in range(3):
            pair_copy(rel, chunk).wait_send()
    for rel in range(3):
        loss_copy(rel).wait_send()
    sib_copy(0).wait_send()
    sib_copy(1).wait_send()
    z_copy.wait_send()


def local_part(student, teacher, band_codes):
    part, width = student.shape
    count = 4 * part
    slots = 2 * REACH + 1
    vmem = pl.BlockSpec(memory_space=pltpu.VMEM)
    anywhere = pl.BlockSpec(memory_space=pl.ANY)
    dma = pltpu.SemaphoreType.DMA
    return pl.pallas_call(
        kernel,
        out_shape=(
            jax.ShapeDtypeStruct((1, 1), jnp.float32),
            jax.ShapeDtypeStruct((part, width), jnp.float32),
        ),
        in_specs=[anywhere, anywhere, pl.BlockSpec(memory_space=pltpu.SMEM)],
        out_specs=(vmem, vmem),
        scratch_shapes=[
            pltpu.VMEM((2 * count, width), jnp.bfloat16),
            pltpu.VMEM((slots, 2 * part, width), jnp.bfloat16),
            pltpu.VMEM((2 * count, 128), jnp.float32),
            pltpu.VMEM((slots, 8, 2 * part), jnp.float32),
            pltpu.VMEM((2 * count, 2 * part), jnp.float32),
            pltpu.VMEM((count, 2 * part), jnp.bfloat16),
            pltpu.VMEM((count, width), jnp.float32),
            pltpu.VMEM((count, part), jnp.float32),
            pltpu.VMEM((4, 8, part), jnp.float32),
            pltpu.VMEM((3, 8, part), jnp.float32),
            pltpu.VMEM((2, part, width), jnp.float32),
            pltpu.VMEM((part, width), jnp.float32),
            pltpu.VMEM((part, width), jnp.float32),
            dma((2, 2)),
            dma((2, REACH, 2)),
            dma((2, REACH, 2)),
            dma((3, 2)),
            dma((3, 2)),
            dma((3,)),
            dma((3,)),
            dma((3,)),
            dma((3,)),
        ],
        compiler_params=pltpu.CompilerParams(
            collective_id=0, has_side_effects=True, vmem_limit_bytes=40 * 1024 * 1024
        ),
    )(student, teacher, band_codes)


def solution(mesh):
    return jax.shard_map(
        local_part,
        mesh=mesh,
        in_specs=(P(("dp", "pair"), None), P(("dp", "pair"), None), P()),
        out_specs=(P("dp", "pair"), P(("dp", "pair"), None)),
        check_vma=False,
    )
```

time: 531 us -> 101 us (0.19)
  the two profiles are of different devices: /device:TPU:57 before, /device:TPU:9 now
where the time goes in v1:
time: 101 us
  Pallas kernels  95.5 us (95%)
  local copies, waits for them, and re-layouts  3.25 us (3%)
  between operations  2.38 us (2%)
    pallas_call x1, Pallas kernels, local_part(): pl.pallas_call(kernel, out_shape=(jax.ShapeDtypeStruct((1, 1), jnp.float3...  95.5 us
    unnamed x7, local copies, waits for them, and re-layouts  3.25 us

profile of v1, /device:TPU:9, one launch (start us, length us, event | category | flops | bytes accessed | tf_op | source)
XLA Modules:
  0.0 101.1 jit_solution(10078098452803303698)
XLA Ops:
  0.6 0.0 copy-start
  0.6 0.9 copy-done
  1.6 0.0 copy-start.1
  1.6 0.9 copy-done.1
  2.5 0.0 copy-start.2
  2.5 0.7 copy-done.2
  3.1 95.5 %shard_map.50 = (f32[1,1]{1,0:T(1,128)}, f32[128,768]{1,0:T(8,128)S(1)}) custom-call(bf16[128,768]{1,0:T(8,128)(2,1)S(1)} %copy-done, bf16[128,768]{1,0:T(8,128)(2,1)S(1)} %copy-done.1, s32[5]{0:T(128)S(1)} %copy-done.2), custom_call_target="tpu_custom_call" | custom-call | tf_op jit(solution)/shard_map/pallas_call | solution.py:250
  99.2 0.7 copy.8
Async XLA Ops:
  0.6 0.9 copy-start
  1.6 0.9 copy-start.1
  2.5 0.7 copy-start.2

commit v2 on v1

v2 whole, which is shorter than its diff:
```python
import jax
import jax.numpy as jnp
from jax import lax
from jax.experimental import pallas as pl
from jax.experimental.pallas import tpu as pltpu
from jax.sharding import PartitionSpec as P

REACH = 3
ROW = 8
CHUNKS = 4
RELAYED = (1, 3)
LOG2E = 1.4426950408889634


def kernel(student, teacher, codes, loss_out, grad_out,
           bb, cbuf, hold, nb, nc, inner, ebuf, elast, acc, rows_acc, loss_acc, loss_in,
           got, z_out, z_in, r_out, r_in,
           local_sem, dp_send, dp_recv, hold_send, hold_recv, pair_send, pair_recv,
           fin_send, fin_recv, loss_send, loss_recv):
    n_dp = lax.axis_size("dp")
    part, width = student.shape
    count = 4 * part
    piece = 2 * part // CHUNKS
    bands = codes.shape[0]
    b = lax.axis_index("dp")
    p = lax.axis_index("pair")
    z_lo = p // 2
    core = p % 2
    sib = z_lo * 2 + (1 - core)
    zp = (1 - z_lo) * 2 + core
    diag = (1 - z_lo) * 2 + (1 - core)
    up = (b + 1) % n_dp
    down = (b + n_dp - 1) % n_dp
    column = b % ROW
    is_top = column == ROW - 1
    is_bottom = column == 0
    up_row = (b + ROW) % n_dp
    down_row = (b + n_dp - ROW) % n_dp
    row_bottom = b - column
    row_top = row_bottom + ROW - 1

    def dev(block, place):
        return {"dp": block, "pair": place}

    def rows_of(q, chunk):
        return pl.ds(pl.multiple_of(chunk * count + q * part, part), part)

    def quarter(q):
        return pl.ds(pl.multiple_of(q * part, part), part)

    barrier = pltpu.get_barrier_semaphore()

    def greet(*targets):
        for target in targets:
            pl.semaphore_signal(barrier, inc=1, device_id=target, device_id_type=pl.DeviceIdType.MESH)

    greet(dev(up, p), dev(down, p), dev(b, sib), dev(b, zp), dev(b, diag))

    @pl.when(is_top)
    def _():
        greet(dev(up_row, p), dev(down_row, p), dev(row_bottom, p))
        pl.semaphore_wait(barrier, 8)

    @pl.when(is_bottom)
    def _():
        greet(dev(up_row, p), dev(down_row, p), dev(row_top, p))
        pl.semaphore_wait(barrier, 8)

    @pl.when(jnp.logical_not(jnp.logical_or(is_top, is_bottom)))
    def _():
        pl.semaphore_wait(barrier, 5)

    own = (student, teacher)

    def remote(src, dst, ssem, rsem, target):
        return pltpu.make_async_remote_copy(
            src_ref=src, dst_ref=dst, send_sem=ssem, recv_sem=rsem,
            device_id=target, device_id_type=pl.DeviceIdType.MESH)

    def own_piece(chunk):
        first = chunk * piece
        return own[first // part].at[pl.ds(first % part, piece)]

    def slot_piece(slot, chunk):
        return cbuf.at[slot, pl.ds(chunk * piece, piece)]

    def dp_copy(way, step, chunk):
        sign = -1 if way == 0 else 1
        src = own_piece(chunk) if step == 1 else slot_piece(REACH + sign * (step - 1), chunk)
        return remote(src, slot_piece(REACH + sign * step, chunk),
                      dp_send.at[way, step - 1, chunk], dp_recv.at[way, step - 1, chunk],
                      dev(up if way == 0 else down, p))

    def hold_copy(way, step, chunk):
        sign = -1 if way == 0 else 1
        src = own_piece(chunk) if step == 1 else slot_piece(REACH + sign * (step - 1), chunk)
        index = RELAYED.index(chunk)
        return remote(src, hold.at[step - 1, index], dp_send.at[way, step - 1, chunk],
                      hold_recv.at[step - 1, index], dev(up_row if way == 0 else down_row, p))

    def pass_copy(way, step, chunk):
        sign = -1 if way == 0 else 1
        index = RELAYED.index(chunk)
        return remote(hold.at[step - 1, index], slot_piece(REACH + sign * step, chunk),
                      hold_send.at[step - 1, index], dp_recv.at[way, step - 1, chunk],
                      dev(row_bottom if way == 0 else row_top, p))

    def dp_start(way, step, chunk):
        if chunk in RELAYED:
            edge = is_top if way == 0 else is_bottom

            @pl.when(edge)
            def _():
                hold_copy(way, step, chunk).start()

            @pl.when(jnp.logical_not(edge))
            def _():
                dp_copy(way, step, chunk).start()
        else:
            dp_copy(way, step, chunk).start()

    def relay(step):
        for way in (0, 1):
            @pl.when(is_top if way == 0 else is_bottom)
            def _():
                for chunk in RELAYED:
                    hold_copy(way, step, chunk).wait_recv()
                    pass_copy(way, step, chunk).start()

    def pair_copy(rel, chunk):
        if rel == 2:
            src = dst = bb.at[rows_of(zp, chunk)]
        else:
            src, dst = own[chunk], bb.at[rows_of(p, chunk)]
        target = dev(b, zp if rel == 1 else sib)
        return remote(src, dst, pair_send.at[rel, chunk], pair_recv.at[rel, chunk], target)

    def pair_arrived(rel, chunk):
        q = (sib, zp, diag)[rel]
        ref = bb.at[rows_of(q, chunk)]
        remote(ref, ref, pair_send.at[rel, chunk], pair_recv.at[rel, chunk], dev(b, sib)).wait_recv()

    local = [pltpu.make_async_copy(own[c], cbuf.at[REACH, pl.ds(c * part, part)], local_sem.at[0, c]) for c in (0, 1)]
    local += [pltpu.make_async_copy(own[c], bb.at[rows_of(p, c)], local_sem.at[1, c]) for c in (0, 1)]
    for chunk in range(CHUNKS):
        for way in (0, 1):
            dp_start(way, 1, chunk)
        if chunk == 1:
            pair_copy(1, 0).start()
            pair_copy(0, 0).start()
    pair_copy(1, 1).start()
    pair_copy(0, 1).start()
    for c in local:
        c.start()

    scale = [2.0 / (codes[m].astype(jnp.float32) * width) for m in range(bands)]
    expo = [s * (-LOG2E) for s in scale]
    factor = 2.0 * width / count
    slope = [s * factor for s in scale]

    acc[...] = jnp.zeros_like(acc)
    rows_acc[...] = jnp.zeros_like(rows_acc)
    loss_acc[...] = jnp.zeros_like(loss_acc)

    def split_squares(x):
        sq = jnp.square(x.astype(jnp.float32))
        hi = sq.astype(jnp.bfloat16)
        lo = (sq - hi.astype(jnp.float32)).astype(jnp.bfloat16)
        return hi, lo

    def nt(x, y):
        return lax.dot_general(x, y, (((1,), (1,)), ((), ())), preferred_element_type=jnp.float32)

    def row_norms(q, chunk):
        here = rows_of(q, chunk)
        hi, lo = split_squares(bb[here, :])
        ones = jnp.ones((128, width), jnp.bfloat16)
        nb[here, :] = nt(hi, ones) + nt(lo, ones)

    step_rows = 32

    def work(offset, parts):
        slot = REACH + offset
        ahead = offset >= 0
        last = abs(offset) == REACH and parts == (1,)
        weight = [2.0 * w for w in slope] if offset == 0 else slope
        first = parts[0] * part
        wide = len(parts) * part
        here_cols = pl.ds(first, wide)
        cols = cbuf[slot, here_cols, :]
        hi, lo = split_squares(cols)
        ones = jnp.ones((8, width), jnp.bfloat16)
        nc[slot, :, here_cols] = nt(ones, hi) + nt(ones, lo)
        inner[pl.ds(0, count), here_cols] = nt(bb[pl.ds(0, count), :], cols)
        if ahead:
            inner[pl.ds(count, count), here_cols] = nt(bb[pl.ds(count, count), :], cols)

        def dist(here, at):
            norm = nb[here, :] + nc[slot, 0:1, pl.ds(at * part, part)]
            return norm - 2.0 * inner[here, pl.ds(at * part, part)]

        def sums(d, want_value, want_slope):
            value = slope_sum = None
            for m in range(bands):
                term = jnp.exp2(d * expo[m])
                if want_value:
                    value = term if value is None else value + term
                if want_slope:
                    scaled = term * weight[m]
                    slope_sum = scaled if slope_sum is None else slope_sum + scaled
            return value, slope_sum

        def fold(x):
            return jnp.sum(x.reshape(step_rows // 8, 8, part), axis=0)

        def body(i, total):
            here = pl.ds(pl.multiple_of(i * step_rows, step_rows), step_rows)
            there = pl.ds(pl.multiple_of(count + i * step_rows, step_rows), step_rows)
            for at in parts:
                value, coeff = sums(dist(here, at), ahead, True)
                if at == 0:
                    ebuf[here, pl.ds(0, part)] = coeff.astype(jnp.bfloat16)
                    rows_acc[here, :] -= coeff
                else:
                    negative = (-coeff).astype(jnp.bfloat16)
                    if last:
                        elast[here, pl.ds(0 if ahead else part, part)] = negative
                    else:
                        ebuf[here, pl.ds(part, part)] = negative
                    rows_acc[here, :] += coeff
                if ahead:
                    other, _ = sums(dist(there, at), True, False)
                    total = total + fold(value - other if at == 0 else other - value)
            return total

        total = lax.fori_loop(0, count // step_rows, body, jnp.zeros((8, part), jnp.float32))
        if ahead:
            loss_acc[offset] += total
        if not last:
            acc[...] += jnp.dot(ebuf[:, here_cols], cols, preferred_element_type=jnp.float32)

    def arrived(step, *chunks):
        for chunk in chunks:
            for way in (0, 1):
                dp_copy(way, step, chunk).wait_recv()
                if step < REACH:
                    dp_start(way, step + 1, chunk)

    for c in local:
        c.wait()
    for chunk in (0, 1):
        row_norms(p, chunk)
        pair_arrived(0, chunk)
        row_norms(sib, chunk)
    relay(1)
    arrived(1, 0, 1, 2, 3)
    for chunk in (0, 1):
        pair_arrived(1, chunk)
        pair_copy(2, chunk).start()
        row_norms(zp, chunk)
    for chunk in (0, 1):
        pair_arrived(2, chunk)
        row_norms(diag, chunk)
    ones = jnp.ones((8, count), jnp.bfloat16)
    centre = jnp.dot(ones, bb[pl.ds(0, count), :], preferred_element_type=jnp.float32)[0:1, :] * (1.0 / count)
    work(0, (0, 1))
    relay(2)
    work(1, (0, 1))
    arrived(2, 0, 1)
    work(-1, (0, 1))
    arrived(2, 2, 3)
    relay(3)
    work(2, (0, 1))
    work(-2, (0, 1))
    arrived(3, 0, 1)
    work(3, (0,))
    work(-3, (0,))
    arrived(3, 2, 3)
    work(3, (1,))
    work(-3, (1,))

    def loss_copy(rel):
        q = (sib, zp, diag)[rel]
        return remote(loss_acc.at[q], loss_in.at[rel], loss_send.at[rel], loss_recv.at[rel], dev(b, q))

    for rel in range(3):
        loss_copy(rel).start()

    tail = jnp.concatenate([cbuf[2 * REACH, pl.ds(part, part), :], cbuf[0, pl.ds(part, part), :]], axis=0)

    def gather_rows(q):
        here = quarter(q)
        products = acc[here, :] + jnp.dot(elast[here, :], tail, preferred_element_type=jnp.float32)
        return products, jnp.sum(rows_acc[here, :], axis=1, keepdims=True)

    def as_row(r):
        return jnp.transpose(jnp.broadcast_to(r, (part, 128)))[0:8, :]

    def sib_copy(which):
        q = (diag, sib)[which]
        return remote(acc.at[quarter(q)], got.at[which], fin_send.at[which], fin_recv.at[which], dev(b, sib))

    sib_row_copy = remote(r_out.at[0], r_in.at[0], fin_send.at[2], fin_recv.at[2], dev(b, sib))
    z_row_copy = remote(r_out.at[1], r_in.at[1], fin_send.at[3], fin_recv.at[3], dev(b, zp))
    z_copy = remote(z_out, z_in, fin_send.at[4], fin_recv.at[4], dev(b, zp))

    products, r = gather_rows(diag)
    acc[quarter(diag), :] = products + r * centre
    r_out[0] = as_row(r)
    sib_row_copy.start()
    sib_copy(0).start()
    products, r = gather_rows(zp)
    acc[quarter(zp), :] = products + r * centre
    r_out[1] = as_row(r)
    products, r = gather_rows(sib)
    acc[quarter(sib), :] = products + r * bb[quarter(sib), :].astype(jnp.float32)
    sib_copy(1).start()
    sib_row_copy.wait_recv()
    r_out[1] += r_in[0]
    z_row_copy.start()
    sib_copy(0).wait_recv()
    z_out[...] = (acc[quarter(zp), :] + got[0]).astype(jnp.bfloat16)
    z_copy.start()
    mine = bb[quarter(p), :].astype(jnp.float32)
    products, r = gather_rows(p)
    grad = products + r * mine
    for rel in range(3):
        loss_copy(rel).wait_recv()
    total = loss_acc[p] + loss_in[0] + loss_in[1] + loss_in[2]
    loss_out[...] = jnp.sum(jnp.sum(total, axis=1, keepdims=True), axis=0, keepdims=True) * (1.0 / count)
    sib_copy(1).wait_recv()
    z_row_copy.wait_recv()
    far = jnp.transpose(jnp.broadcast_to(r_in[1, 0:1, :], (128, part)))[:, 0:1]
    grad = grad + got[1] + far * (mine - centre)
    z_copy.wait_recv()
    grad_out[...] = grad + z_in[...].astype(jnp.float32)

    for chunk in range(CHUNKS):
        for way in (0, 1):
            for step in range(1, REACH + 1):
                dp_copy(way, step, chunk).wait_send()
    for way in (0, 1):
        @pl.when(is_top if way == 0 else is_bottom)
        def _():
            for step in range(1, REACH + 1):
                for chunk in RELAYED:
                    pass_copy(way, step, chunk).wait_send()
    for chunk in (0, 1):
        for rel in range(3):
            pair_copy(rel, chunk).wait_send()
    for rel in range(3):
        loss_copy(rel).wait_send()
    sib_copy(0).wait_send()
    sib_copy(1).wait_send()
    sib_row_copy.wait_send()
    z_row_copy.wait_send()
    z_copy.wait_send()


def local_part(student, teacher, band_codes):
    part, width = student.shape
    count = 4 * part
    slots = 2 * REACH + 1
    piece = 2 * part // CHUNKS
    relayed = len(RELAYED)
    vmem = pl.BlockSpec(memory_space=pltpu.VMEM)
    anywhere = pl.BlockSpec(memory_space=pl.ANY)
    dma = pltpu.SemaphoreType.DMA
    return pl.pallas_call(
        kernel,
        out_shape=(
            jax.ShapeDtypeStruct((1, 1), jnp.float32),
            jax.ShapeDtypeStruct((part, width), jnp.float32),
        ),
        in_specs=[anywhere, anywhere, pl.BlockSpec(memory_space=pltpu.SMEM)],
        out_specs=(vmem, vmem),
        scratch_shapes=[
            pltpu.VMEM((2 * count, width), jnp.bfloat16),
            pltpu.VMEM((slots, 2 * part, width), jnp.bfloat16),
            pltpu.VMEM((REACH, relayed, piece, width), jnp.bfloat16),
            pltpu.VMEM((2 * count, 128), jnp.float32),
            pltpu.VMEM((slots, 8, 2 * part), jnp.float32),
            pltpu.VMEM((2 * count, 2 * part), jnp.float32),
            pltpu.VMEM((count, 2 * part), jnp.bfloat16),
            pltpu.VMEM((count, 2 * part), jnp.bfloat16),
            pltpu.VMEM((count, width), jnp.float32),
            pltpu.VMEM((count, part), jnp.float32),
            pltpu.VMEM((REACH + 1, 8, part), jnp.float32),
            pltpu.VMEM((3, 8, part), jnp.float32),
            pltpu.VMEM((2, part, width), jnp.float32),
            pltpu.VMEM((part, width), jnp.bfloat16),
            pltpu.VMEM((part, width), jnp.bfloat16),
            pltpu.VMEM((2, 8, 128), jnp.float32),
            pltpu.VMEM((2, 8, 128), jnp.float32),
            dma((2, 2)),
            dma((2, REACH, CHUNKS)),
            dma((2, REACH, CHUNKS)),
            dma((REACH, relayed)),
            dma((REACH, relayed)),
            dma((3, 2)),
            dma((3, 2)),
            dma((5,)),
            dma((5,)),
            dma((3,)),
            dma((3,)),
        ],
        compiler_params=pltpu.CompilerParams(
            collective_id=0, has_side_effects=True, vmem_limit_bytes=60 * 1024 * 1024
        ),
    )(student, teacher, band_codes)


def solution(mesh):
    return jax.shard_map(
        local_part,
        mesh=mesh,
        in_specs=(P(("dp", "pair"), None), P(("dp", "pair"), None), P()),
        out_specs=(P("dp", "pair"), P(("dp", "pair"), None)),
        check_vma=False,
    )
```

time: 101 us -> 80.6 us (0.80)
  the two profiles are of different devices: /device:TPU:9 before, /device:TPU:57 now
where the time goes in v2:
time: 80.6 us; the launch traced here: 80.4 us
  Pallas kernels  76.3 us (95%)
  between operations  2.39 us (3%)
  local copies, waits for them, and re-layouts  1.77 us (2%)
    pallas_call x1, Pallas kernels, local_part(): pl.pallas_call(kernel, out_shape=(jax.ShapeDtypeStruct((1, 1), jnp.float3...  76.3 us
    unnamed x1, local copies, waits for them, and re-layouts  1.77 us

profile of v2, /device:TPU:57, one launch (start us, length us, event | category | flops | bytes accessed | tf_op | source)
XLA Modules:
  0.0 80.4 jit_solution(2655387178894775428)
XLA Ops:
  0.6 76.3 %shard_map.50 = (f32[1,1]{1,0:T(1,128)}, f32[128,768]{1,0:T(8,128)}) custom-call(bf16[128,768]{1,0:T(8,128)(2,1)} %student.1, bf16[128,768]{1,0:T(8,128)(2,1)} %teacher.1, s32[5]{0:T(128)} %codes.1), custom_call_target="tpu_custom_call" | custom-call | tf_op jit(solution)/shard_map/pallas_call | solution.py:369
  77.5 1.8 %copy.8 = f32[128,768]{1,0:T(8,128)} copy(f32[128,768]{1,0:T(8,128)} %get-tuple-element.5) | data formatting | bytes 786432

commit v3 on v2

--- a/solution.py
+++ b/solution.py
@@ -9,13 +9,14 @@
 ROW = 8
 CHUNKS = 4
 RELAYED = (1, 3)
+SIDE = (0, 1)
 LOG2E = 1.4426950408889634
 
 
 def kernel(student, teacher, codes, loss_out, grad_out,
-           bb, cbuf, hold, nb, nc, inner, ebuf, elast, acc, rows_acc, loss_acc, loss_in,
+           bb, cbuf, hold, side_hold, nb, nc, inner, ebuf, elast, acc, rows_acc, loss_acc, loss_in,
            got, z_out, z_in, r_out, r_in,
-           local_sem, dp_send, dp_recv, hold_send, hold_recv, pair_send, pair_recv,
+           local_sem, dp_send, dp_recv, hold_send, hold_recv, side_send, side_recv, side_pass, pair_send, pair_recv,
            fin_send, fin_recv, loss_send, loss_recv):
     n_dp = lax.axis_size("dp")
     part, width = student.shape
@@ -55,18 +56,32 @@
             pl.semaphore_signal(barrier, inc=1, device_id=target, device_id_type=pl.DeviceIdType.MESH)
 
     greet(dev(up, p), dev(down, p), dev(b, sib), dev(b, zp), dev(b, diag))
+    near_top = column == ROW - 2
+    near_bottom = column == 1
+    is_edge = jnp.logical_or(is_top, is_bottom)
+    is_next = jnp.logical_or(near_top, near_bottom)
 
     @pl.when(is_top)
+    def _():
+        greet(dev(up_row, p), dev(down_row, p), dev(row_bottom, p), dev(row_bottom + 1, p))
+        pl.semaphore_wait(barrier, 9)
+
+    @pl.when(is_bottom)
+    def _():
+        greet(dev(up_row, p), dev(down_row, p), dev(row_top, p), dev(row_top - 1, p))
+        pl.semaphore_wait(barrier, 9)
+
+    @pl.when(near_top)
     def _():
         greet(dev(up_row, p), dev(down_row, p), dev(row_bottom, p))
         pl.semaphore_wait(barrier, 8)
 
-    @pl.when(is_bottom)
+    @pl.when(near_bottom)
     def _():
         greet(dev(up_row, p), dev(down_row, p), dev(row_top, p))
         pl.semaphore_wait(barrier, 8)
 
-    @pl.when(jnp.logical_not(jnp.logical_or(is_top, is_bottom)))
+    @pl.when(jnp.logical_not(jnp.logical_or(is_edge, is_next)))
     def _():
         pl.semaphore_wait(barrier, 5)
 
@@ -105,13 +120,26 @@
                       hold_send.at[step - 1, index], dp_recv.at[way, step - 1, chunk],
                       dev(row_bottom if way == 0 else row_top, p))
 
+    def side_copy(way, chunk):
+        sign = -1 if way == 0 else 1
+        index = SIDE.index(chunk)
+        return remote(slot_piece(REACH + sign, chunk), side_hold.at[index], side_send.at[index], side_recv.at[index],
+                      dev(up_row if way == 0 else down_row, p))
+
+    def side_pass_copy(way, chunk):
+        sign = -1 if way == 0 else 1
+        index = SIDE.index(chunk)
+        return remote(side_hold.at[index], slot_piece(REACH + sign * REACH, chunk), side_pass.at[index],
+                      dp_recv.at[way, REACH - 1, chunk], dev(row_bottom if way == 0 else row_top, p))
+
     def dp_start(way, step, chunk):
-        if chunk in RELAYED:
-            edge = is_top if way == 0 else is_bottom
-
-            @pl.when(edge)
-            def _():
-                hold_copy(way, step, chunk).start()
+        edge = is_top if way == 0 else is_bottom
+        by_side = step == REACH and chunk in SIDE
+        if by_side or chunk in RELAYED:
+            if not by_side:
+                @pl.when(edge)
+                def _():
+                    hold_copy(way, step, chunk).start()
 
             @pl.when(jnp.logical_not(edge))
             def _():
@@ -119,13 +147,80 @@
         else:
             dp_copy(way, step, chunk).start()
 
-    def relay(step):
-        for way in (0, 1):
-            @pl.when(is_top if way == 0 else is_bottom)
-            def _():
-                for chunk in RELAYED:
-                    hold_copy(way, step, chunk).wait_recv()
-                    pass_copy(way, step, chunk).start()
+    def relay(way, step, *chunks):
+        for chunk in chunks:
+            hold_copy(way, step, chunk).wait_recv()
+            pass_copy(way, step, chunk).start()
+
+    def side_relay(way):
+        for chunk in SIDE:
+            side_copy(way, chunk).wait_recv()
+            side_pass_copy(way, chunk).start()
+
+    def take(way, step, *chunks):
+        for chunk in chunks:
+            dp_copy(way, step, chunk).wait_recv()
+            if step < REACH:
+                dp_start(way, step + 1, chunk)
+
+    high = column >= ROW // 2
+    everything = tuple(range(CHUNKS))
+    straight = tuple(c for c in everything if c not in RELAYED)
+    relayed_last = tuple(c for c in RELAYED if c not in SIDE)
+
+    def by_kind(edge_order, next_order, inner_order):
+        for near in (0, 1):
+            far = 1 - near
+            for chosen, order in ((is_edge, edge_order), (is_next, next_order),
+                                  (jnp.logical_not(jnp.logical_or(is_edge, is_next)), inner_order)):
+                @pl.when(jnp.logical_and(chosen, high if near == 0 else jnp.logical_not(high)))
+                def _():
+                    order(near, far)
+
+    def edge_first(near, far):
+        take(near, 1, 0, 1)
+        relay(near, 1, RELAYED[0])
+        take(near, 1, 2, 3)
+        relay(near, 1, RELAYED[1])
+        take(far, 1, *straight)
+
+    def next_first(near, far):
+        for chunk in everything:
+            take(near, 1, chunk)
+            if chunk in SIDE:
+                side_copy(near, chunk).start()
+            take(far, 1, chunk)
+
+    def inner_first(near, far):
+        for chunk in everything:
+            take(near, 1, chunk)
+            take(far, 1, chunk)
+
+    def edge_second(near, far):
+        take(far, 1, *RELAYED)
+
+    def next_second(near, far):
+        side_relay(near)
+
+    def nothing(near, far):
+        pass
+
+    def edge_third(near, far):
+        take(near, 2, 0, 1)
+        relay(near, 2, RELAYED[0])
+        take(near, 2, 2, 3)
+        relay(near, 2, RELAYED[1])
+
+    def inner_third(near, far):
+        take(near, 2, *everything)
+
+    def edge_fourth(near, far):
+        take(far, 2, *straight)
+        take(far, 2, *RELAYED)
+        relay(near, 3, *relayed_last)
+
+    def inner_fourth(near, far):
+        take(far, 2, *everything)
 
     def pair_copy(rel, chunk):
         if rel == 2:
@@ -179,24 +274,38 @@
 
     step_rows = 32
 
-    def work(offset, parts):
+    def col_norms(offset, parts):
+        slot = REACH + offset
+        here = pl.ds(parts[0] * part, len(parts) * part)
+        hi, lo = split_squares(cbuf[slot, here, :])
+        ones = jnp.ones((8, width), jnp.bfloat16)
+        nc[slot, :, here] = nt(ones, hi) + nt(ones, lo)
+
+    chip_rows = 2 * part
+
+    def work(offset, parts, chip=None):
         slot = REACH + offset
         ahead = offset >= 0
         last = abs(offset) == REACH and parts == (1,)
         weight = [2.0 * w for w in slope] if offset == 0 else slope
-        first = parts[0] * part
-        wide = len(parts) * part
-        here_cols = pl.ds(first, wide)
+        here_cols = pl.ds(parts[0] * part, len(parts) * part)
+        if chip is None:
+            base, rows = 0, count
+        else:
+            base, rows = (z_lo if chip == 0 else 1 - z_lo) * chip_rows, chip_rows
+        if chip != 1:
+            col_norms(offset, parts)
         cols = cbuf[slot, here_cols, :]
-        hi, lo = split_squares(cols)
-        ones = jnp.ones((8, width), jnp.bfloat16)
-        nc[slot, :, here_cols] = nt(ones, hi) + nt(ones, lo)
-        inner[pl.ds(0, count), here_cols] = nt(bb[pl.ds(0, count), :], cols)
+
+        def block(first, size):
+            return pl.ds(pl.multiple_of(base + first, size), size)
+
+        inner[pl.ds(0, rows), here_cols] = nt(bb[block(0, rows), :], cols)
         if ahead:
-            inner[pl.ds(count, count), here_cols] = nt(bb[pl.ds(count, count), :], cols)
-
-        def dist(here, at):
-            norm = nb[here, :] + nc[slot, 0:1, pl.ds(at * part, part)]
+            inner[pl.ds(count, rows), here_cols] = nt(bb[block(count, rows), :], cols)
+
+        def dist(norm_rows, here, at):
+            norm = nb[norm_rows, :] + nc[slot, 0:1, pl.ds(at * part, part)]
             return norm - 2.0 * inner[here, pl.ds(at * part, part)]
 
         def sums(d, want_value, want_slope):
@@ -216,35 +325,31 @@
         def body(i, total):
             here = pl.ds(pl.multiple_of(i * step_rows, step_rows), step_rows)
             there = pl.ds(pl.multiple_of(count + i * step_rows, step_rows), step_rows)
+            block_here = block(i * step_rows, step_rows)
+            block_there = block(count + i * step_rows, step_rows)
             for at in parts:
-                value, coeff = sums(dist(here, at), ahead, True)
+                value, coeff = sums(dist(block_here, here, at), ahead, True)
                 if at == 0:
                     ebuf[here, pl.ds(0, part)] = coeff.astype(jnp.bfloat16)
-                    rows_acc[here, :] -= coeff
+                    rows_acc[block_here, :] -= coeff
                 else:
                     negative = (-coeff).astype(jnp.bfloat16)
                     if last:
-                        elast[here, pl.ds(0 if ahead else part, part)] = negative
+                        elast[here, :] = negative
                     else:
                         ebuf[here, pl.ds(part, part)] = negative
-                    rows_acc[here, :] += coeff
+                    rows_acc[block_here, :] += coeff
                 if ahead:
-                    other, _ = sums(dist(there, at), True, False)
+                    other, _ = sums(dist(block_there, there, at), True, False)
                     total = total + fold(value - other if at == 0 else other - value)
             return total
 
-        total = lax.fori_loop(0, count // step_rows, body, jnp.zeros((8, part), jnp.float32))
+        total = lax.fori_loop(0, rows // step_rows, body, jnp.zeros((8, part), jnp.float32))
         if ahead:
             loss_acc[offset] += total
         if not last:
-            acc[...] += jnp.dot(ebuf[:, here_cols], cols, preferred_element_type=jnp.float32)
-
-    def arrived(step, *chunks):
-        for chunk in chunks:
-            for way in (0, 1):
-                dp_copy(way, step, chunk).wait_recv()
-                if step < REACH:
-                    dp_start(way, step + 1, chunk)
+            acc[block(0, rows), :] += jnp.dot(
+                ebuf[pl.ds(0, rows), here_cols], cols, preferred_element_type=jnp.float32)
 
     for c in local:
         c.wait()
@@ -252,32 +357,38 @@
         row_norms(p, chunk)
         pair_arrived(0, chunk)
         row_norms(sib, chunk)
-    relay(1)
-    arrived(1, 0, 1, 2, 3)
+    both = (0, 1)
+    by_kind(edge_first, next_first, inner_first)
+    work(0, both, 0)
+    by_kind(edge_second, next_second, nothing)
+    work(1, both, 0)
+    work(-1, both, 0)
+    by_kind(edge_third, inner_third, inner_third)
     for chunk in (0, 1):
         pair_arrived(1, chunk)
         pair_copy(2, chunk).start()
         row_norms(zp, chunk)
+    ones = jnp.ones((8, count), jnp.bfloat16)
     for chunk in (0, 1):
         pair_arrived(2, chunk)
         row_norms(diag, chunk)
-    ones = jnp.ones((8, count), jnp.bfloat16)
     centre = jnp.dot(ones, bb[pl.ds(0, count), :], preferred_element_type=jnp.float32)[0:1, :] * (1.0 / count)
-    work(0, (0, 1))
-    relay(2)
-    work(1, (0, 1))
-    arrived(2, 0, 1)
-    work(-1, (0, 1))
-    arrived(2, 2, 3)
-    relay(3)
-    work(2, (0, 1))
-    work(-2, (0, 1))
-    arrived(3, 0, 1)
-    work(3, (0,))
-    work(-3, (0,))
-    arrived(3, 2, 3)
-    work(3, (1,))
-    work(-3, (1,))
+    work(0, both, 1)
+    work(1, both, 1)
+    work(-1, both, 1)
+    by_kind(edge_fourth, inner_fourth, inner_fourth)
+    work(2, both)
+    work(-2, both)
+    for near in (0, 1):
+        @pl.when(high if near == 0 else jnp.logical_not(high))
+        def _():
+            near_offset = -REACH if near == 0 else REACH
+            take(near, REACH, *everything)
+            work(near_offset, both)
+            take(1 - near, REACH, 0, 1)
+            work(-near_offset, (0,))
+            take(1 - near, REACH, 2, 3)
+            work(-near_offset, (1,))
 
     def loss_copy(rel):
         q = (sib, zp, diag)[rel]
@@ -286,7 +397,7 @@
     for rel in range(3):
         loss_copy(rel).start()
 
-    tail = jnp.concatenate([cbuf[2 * REACH, pl.ds(part, part), :], cbuf[0, pl.ds(part, part), :]], axis=0)
+    tail = cbuf[jnp.where(high, 2 * REACH, 0), pl.ds(part, part), :]
 
     def gather_rows(q):
         here = quarter(q)
@@ -338,13 +449,24 @@
     for chunk in range(CHUNKS):
         for way in (0, 1):
             for step in range(1, REACH + 1):
-                dp_copy(way, step, chunk).wait_send()
+                if step == REACH and chunk in SIDE:
+                    @pl.when(jnp.logical_not(is_top if way == 0 else is_bottom))
+                    def _():
+                        dp_copy(way, step, chunk).wait_send()
+                else:
+                    dp_copy(way, step, chunk).wait_send()
     for way in (0, 1):
         @pl.when(is_top if way == 0 else is_bottom)
         def _():
             for step in range(1, REACH + 1):
-                for chunk in RELAYED:
+                for chunk in RELAYED if step < REACH else relayed_last:
                     pass_copy(way, step, chunk).wait_send()
+
+        @pl.when(near_top if way == 0 else near_bottom)
+        def _():
+            for chunk in SIDE:
+                side_copy(way, chunk).wait_send()
+                side_pass_copy(way, chunk).wait_send()
     for chunk in (0, 1):
         for rel in range(3):
             pair_copy(rel, chunk).wait_send()
@@ -378,11 +500,12 @@
             pltpu.VMEM((2 * count, width), jnp.bfloat16),
             pltpu.VMEM((slots, 2 * part, width), jnp.bfloat16),
             pltpu.VMEM((REACH, relayed, piece, width), jnp.bfloat16),
+            pltpu.VMEM((len(SIDE), piece, width), jnp.bfloat16),
             pltpu.VMEM((2 * count, 128), jnp.float32),
             pltpu.VMEM((slots, 8, 2 * part), jnp.float32),
             pltpu.VMEM((2 * count, 2 * part), jnp.float32),
             pltpu.VMEM((count, 2 * part), jnp.bfloat16),
-            pltpu.VMEM((count, 2 * part), jnp.bfloat16),
+            pltpu.VMEM((count, part), jnp.bfloat16),
             pltpu.VMEM((count, width), jnp.float32),
             pltpu.VMEM((count, part), jnp.float32),
             pltpu.VMEM((REACH + 1, 8, part), jnp.float32),
@@ -397,6 +520,9 @@
             dma((2, REACH, CHUNKS)),
             dma((REACH, relayed)),
             dma((REACH, relayed)),
+            dma((len(SIDE),)),
+            dma((len(SIDE),)),
+            dma((len(SIDE),)),
             dma((3, 2)),
             dma((3, 2)),
             dma((5,)),

time: 80.6 us -> 72.7 us (0.902)
  Pallas kernels: 76.3 us -> 68.1 us
    pallas_call x1, Pallas kernels: 76.3 us -> 68.1 us  [local_part(): pl.pallas_call(kernel, out_shape=(jax.ShapeDtypeStruct((1, 1), jnp.float3...]
where the time goes in v3:
time: 72.7 us; the launch traced here: 72.3 us
  Pallas kernels  68.1 us (94%)
  between operations  2.39 us (3%)
  local copies, waits for them, and re-layouts  1.77 us (2%)
    pallas_call x1, Pallas kernels, local_part(): pl.pallas_call(kernel, out_shape=(jax.ShapeDtypeStruct((1, 1), jnp.float3...  68.1 us
    unnamed x1, local copies, waits for them, and re-layouts  1.77 us

profile of v3, /device:TPU:57, one launch (start us, length us, event | category | flops | bytes accessed | tf_op | source)
XLA Modules:
  0.0 72.3 jit_solution(17835167475368439668)
XLA Ops:
  0.6 68.1 %shard_map.50 = (f32[1,1]{1,0:T(1,128)}, f32[128,768]{1,0:T(8,128)}) custom-call(bf16[128,768]{1,0:T(8,128)(2,1)} %student.1, bf16[128,768]{1,0:T(8,128)(2,1)} %teacher.1, s32[5]{0:T(128)} %codes.1), custom_call_target="tpu_custom_call" | custom-call | tf_op jit(solution)/shard_map/pallas_call | solution.py:491
  69.4 1.8 %copy.8 = f32[128,768]{1,0:T(8,128)} copy(f32[128,768]{1,0:T(8,128)} %get-tuple-element.5) | data formatting | bytes 786432

commit v4 on v3

--- a/solution.py
+++ b/solution.py
@@ -187,9 +187,9 @@
     def next_first(near, far):
         for chunk in everything:
             take(near, 1, chunk)
-            if chunk in SIDE:
-                side_copy(near, chunk).start()
             take(far, 1, chunk)
+        for chunk in SIDE:
+            side_copy(near, chunk).start()
 
     def inner_first(near, far):
         for chunk in everything:
@@ -211,15 +211,24 @@
         take(near, 2, 2, 3)
         relay(near, 2, RELAYED[1])
 
+    def next_third(near, far):
+        take(near, 2, *everything)
+
     def inner_third(near, far):
-        take(near, 2, *everything)
+        for chunk in everything:
+            take(near, 2, chunk)
+            take(far, 2, chunk)
 
     def edge_fourth(near, far):
         take(far, 2, *straight)
+
+    def edge_fifth(near, far):
         take(far, 2, *RELAYED)
+
+    def edge_sixth(near, far):
         relay(near, 3, *relayed_last)
 
-    def inner_fourth(near, far):
+    def next_fourth(near, far):
         take(far, 2, *everything)
 
     def pair_copy(rel, chunk):
@@ -272,14 +281,17 @@
         ones = jnp.ones((128, width), jnp.bfloat16)
         nb[here, :] = nt(hi, ones) + nt(lo, ones)
 
-    step_rows = 32
+    step_rows = 128
 
     def col_norms(offset, parts):
         slot = REACH + offset
         here = pl.ds(parts[0] * part, len(parts) * part)
-        hi, lo = split_squares(cbuf[slot, here, :])
-        ones = jnp.ones((8, width), jnp.bfloat16)
-        nc[slot, :, here] = nt(ones, hi) + nt(ones, lo)
+        sq = jnp.square(cbuf[slot, here, :].astype(jnp.float32))
+        folded = sq[:, 0:128]
+        for k in range(1, width // 128):
+            folded = folded + sq[:, k * 128:(k + 1) * 128]
+        norms = jnp.sum(jnp.transpose(folded), axis=0, keepdims=True)
+        nc[slot, :, here] = jnp.broadcast_to(norms, (8, len(parts) * part))
 
     chip_rows = 2 * part
 
@@ -358,12 +370,37 @@
         pair_arrived(0, chunk)
         row_norms(sib, chunk)
     both = (0, 1)
+
+    def by_side(order):
+        for near in (0, 1):
+            @pl.when(high if near == 0 else jnp.logical_not(high))
+            def _():
+                order(near, 1 - near, -1 if near == 0 else 1)
+
+    def near_second(near, far, sign):
+        work(2 * sign, both, 0)
+
+    def near_second_other(near, far, sign):
+        work(2 * sign, both, 1)
+
+    def near_third(near, far, sign):
+        take(near, REACH, *everything)
+        work(REACH * sign, both)
+
+    def rest(near, far, sign):
+        work(-2 * sign, both)
+        take(far, REACH, 0, 1)
+        work(-REACH * sign, (0,))
+        take(far, REACH, 2, 3)
+        work(-REACH * sign, (1,))
+
     by_kind(edge_first, next_first, inner_first)
     work(0, both, 0)
     by_kind(edge_second, next_second, nothing)
     work(1, both, 0)
     work(-1, both, 0)
-    by_kind(edge_third, inner_third, inner_third)
+    by_kind(edge_third, next_third, inner_third)
+    by_side(near_second)
     for chunk in (0, 1):
         pair_arrived(1, chunk)
         pair_copy(2, chunk).start()
@@ -374,21 +411,14 @@
         row_norms(diag, chunk)
     centre = jnp.dot(ones, bb[pl.ds(0, count), :], preferred_element_type=jnp.float32)[0:1, :] * (1.0 / count)
     work(0, both, 1)
+    by_kind(edge_fourth, next_fourth, nothing)
     work(1, both, 1)
+    by_kind(edge_fifth, nothing, nothing)
     work(-1, both, 1)
-    by_kind(edge_fourth, inner_fourth, inner_fourth)
-    work(2, both)
-    work(-2, both)
-    for near in (0, 1):
-        @pl.when(high if near == 0 else jnp.logical_not(high))
-        def _():
-            near_offset = -REACH if near == 0 else REACH
-            take(near, REACH, *everything)
-            work(near_offset, both)
-            take(1 - near, REACH, 0, 1)
-            work(-near_offset, (0,))
-            take(1 - near, REACH, 2, 3)
-            work(-near_offset, (1,))
+    by_kind(edge_sixth, nothing, nothing)
+    by_side(near_second_other)
+    by_side(near_third)
+    by_side(rest)
 
     def loss_copy(rel):
         q = (sib, zp, diag)[rel]

time: 72.7 us -> 70.5 us (0.970)
  Pallas kernels: 68.1 us -> 66.1 us
    pallas_call x1, Pallas kernels: 68.1 us -> 66.1 us  [local_part(): pl.pallas_call(kernel, out_shape=(jax.ShapeDtypeStruct((1, 1), jnp.float3...]
where the time goes in v4:
time: 70.5 us; the launch traced here: 70.2 us
  Pallas kernels  66.1 us (94%)
  between operations  2.39 us (3%)
  local copies, waits for them, and re-layouts  1.77 us (3%)
    pallas_call x1, Pallas kernels, local_part(): pl.pallas_call(kernel, out_shape=(jax.ShapeDtypeStruct((1, 1), jnp.float3...  66.1 us
    unnamed x1, local copies, waits for them, and re-layouts  1.77 us

profile of v4, /device:TPU:57, one launch (start us, length us, event | category | flops | bytes accessed | tf_op | source)
XLA Modules:
  0.0 70.2 jit_solution(5042906899293900943)
XLA Ops:
  0.6 66.1 %shard_map.50 = (f32[1,1]{1,0:T(1,128)}, f32[128,768]{1,0:T(8,128)}) custom-call(bf16[128,768]{1,0:T(8,128)(2,1)} %student.1, bf16[128,768]{1,0:T(8,128)(2,1)} %teacher.1, s32[5]{0:T(128)} %codes.1), custom_call_target="tpu_custom_call" | custom-call | tf_op jit(solution)/shard_map/pallas_call | solution.py:521
  67.3 1.8 %copy.8 = f32[128,768]{1,0:T(8,128)} copy(f32[128,768]{1,0:T(8,128)} %get-tuple-element.5) | data formatting | bytes 786432

commit v5 on v4

--- a/solution.py
+++ b/solution.py
@@ -252,7 +252,6 @@
         if chunk == 1:
             pair_copy(1, 0).start()
             pair_copy(0, 0).start()
-    pair_copy(1, 1).start()
     pair_copy(0, 1).start()
     for c in local:
         c.start()
@@ -313,7 +312,10 @@
             return pl.ds(pl.multiple_of(base + first, size), size)
 
         inner[pl.ds(0, rows), here_cols] = nt(bb[block(0, rows), :], cols)
-        if ahead:
+        if offset == 0:
+            teacher_cols = pl.ds(part, part)
+            inner[pl.ds(count, rows), teacher_cols] = nt(bb[block(count, rows), :], cols[part:, :])
+        elif ahead:
             inner[pl.ds(count, rows), here_cols] = nt(bb[block(count, rows), :], cols)
 
         def dist(norm_rows, here, at):
@@ -351,8 +353,12 @@
                     else:
                         ebuf[here, pl.ds(part, part)] = negative
                     rows_acc[block_here, :] += coeff
-                if ahead:
+                if offset == 0 and at == 0:
+                    total = total + fold(value)
+                elif ahead:
                     other, _ = sums(dist(block_there, there, at), True, False)
+                    if offset == 0:
+                        value = 2.0 * value
                     total = total + fold(value - other if at == 0 else other - value)
             return total
 
@@ -387,14 +393,17 @@
         take(near, REACH, *everything)
         work(REACH * sign, both)
 
+    def far_second(near, far, sign):
+        work(-2 * sign, both)
+
     def rest(near, far, sign):
-        work(-2 * sign, both)
         take(far, REACH, 0, 1)
         work(-REACH * sign, (0,))
         take(far, REACH, 2, 3)
         work(-REACH * sign, (1,))
 
     by_kind(edge_first, next_first, inner_first)
+    pair_copy(1, 1).start()
     work(0, both, 0)
     by_kind(edge_second, next_second, nothing)
     work(1, both, 0)
@@ -410,14 +419,15 @@
         pair_arrived(2, chunk)
         row_norms(diag, chunk)
     centre = jnp.dot(ones, bb[pl.ds(0, count), :], preferred_element_type=jnp.float32)[0:1, :] * (1.0 / count)
+    by_kind(edge_fourth, next_fourth, nothing)
     work(0, both, 1)
-    by_kind(edge_fourth, next_fourth, nothing)
     work(1, both, 1)
     by_kind(edge_fifth, nothing, nothing)
     work(-1, both, 1)
     by_kind(edge_sixth, nothing, nothing)
     by_side(near_second_other)
     by_side(near_third)
+    by_side(far_second)
     by_side(rest)
 
     def loss_copy(rel):

time: 70.5 us -> 68.6 us (0.973)
  Pallas kernels: 66.1 us -> 64.2 us
    pallas_call x1, Pallas kernels: 66.1 us -> 64.2 us  [local_part(): pl.pallas_call(kernel, out_shape=(jax.ShapeDtypeStruct((1, 1), jnp.float3...]
where the time goes in v5:
time: 68.6 us; the launch traced here: 68.4 us
  Pallas kernels  64.2 us (94%)
  between operations  2.39 us (3%)
  local copies, waits for them, and re-layouts  1.77 us (3%)
    pallas_call x1, Pallas kernels, local_part(): pl.pallas_call(kernel, out_shape=(jax.ShapeDtypeStruct((1, 1), jnp.float3...  64.2 us
    unnamed x1, local copies, waits for them, and re-layouts  1.77 us

profile of v5, /device:TPU:57, one launch (start us, length us, event | category | flops | bytes accessed | tf_op | source)
XLA Modules:
  0.0 68.4 jit_solution(11536576635983211427)
XLA Ops:
  0.6 64.2 %shard_map.50 = (f32[1,1]{1,0:T(1,128)}, f32[128,768]{1,0:T(8,128)}) custom-call(bf16[128,768]{1,0:T(8,128)(2,1)} %student.1, bf16[128,768]{1,0:T(8,128)(2,1)} %teacher.1, s32[5]{0:T(128)} %codes.1), custom_call_target="tpu_custom_call" | custom-call | tf_op jit(solution)/shard_map/pallas_call | solution.py:531
  65.5 1.8 %copy.8 = f32[128,768]{1,0:T(8,128)} copy(f32[128,768]{1,0:T(8,128)} %get-tuple-element.5) | data formatting | bytes 786432

commit v6 on v5

--- a/solution.py
+++ b/solution.py
@@ -13,7 +13,7 @@
 LOG2E = 1.4426950408889634
 
 
-def kernel(student, teacher, codes, loss_out, grad_out,
+def kernel(student, teacher, codes, loss_out, grad_out, far_out,
            bb, cbuf, hold, side_hold, nb, nc, inner, ebuf, elast, acc, rows_acc, loss_acc, loss_in,
            got, z_out, z_in, r_out, r_in,
            local_sem, dp_send, dp_recv, hold_send, hold_recv, side_send, side_recv, side_pass, pair_send, pair_recv,
@@ -182,7 +182,6 @@
         relay(near, 1, RELAYED[0])
         take(near, 1, 2, 3)
         relay(near, 1, RELAYED[1])
-        take(far, 1, *straight)
 
     def next_first(near, far):
         for chunk in everything:
@@ -197,6 +196,7 @@
             take(far, 1, chunk)
 
     def edge_second(near, far):
+        take(far, 1, *straight)
         take(far, 1, *RELAYED)
 
     def next_second(near, far):
@@ -483,8 +483,9 @@
     z_row_copy.wait_recv()
     far = jnp.transpose(jnp.broadcast_to(r_in[1, 0:1, :], (128, part)))[:, 0:1]
     grad = grad + got[1] + far * (mine - centre)
+    grad_out[...] = grad
     z_copy.wait_recv()
-    grad_out[...] = grad + z_in[...].astype(jnp.float32)
+    far_out[...] = z_in[...]
 
     for chunk in range(CHUNKS):
         for way in (0, 1):
@@ -528,14 +529,15 @@
     vmem = pl.BlockSpec(memory_space=pltpu.VMEM)
     anywhere = pl.BlockSpec(memory_space=pl.ANY)
     dma = pltpu.SemaphoreType.DMA
-    return pl.pallas_call(
+    loss, near, far = pl.pallas_call(
         kernel,
         out_shape=(
             jax.ShapeDtypeStruct((1, 1), jnp.float32),
             jax.ShapeDtypeStruct((part, width), jnp.float32),
+            jax.ShapeDtypeStruct((part, width), jnp.bfloat16),
         ),
         in_specs=[anywhere, anywhere, pl.BlockSpec(memory_space=pltpu.SMEM)],
-        out_specs=(vmem, vmem),
+        out_specs=(vmem, vmem, vmem),
         scratch_shapes=[
             pltpu.VMEM((2 * count, width), jnp.bfloat16),
             pltpu.VMEM((slots, 2 * part, width), jnp.bfloat16),
@@ -574,6 +576,7 @@
             collective_id=0, has_side_effects=True, vmem_limit_bytes=60 * 1024 * 1024
         ),
     )(student, teacher, band_codes)
+    return loss, near + far.astype(jnp.float32)
 
 
 def solution(mesh):

time: 68.6 us -> 68.8 us (level)
  other arithmetic: 0 us -> 1.83 us
  local copies, waits for them, and re-layouts: 1.77 us -> 0 us
    add x0 -> x1, other arithmetic: none -> 1.83 us  [local_part(): return (loss, near + far.astype(jnp.float32))]
    unnamed x1 -> x0, local copies, waits for them, and re-layouts: 1.77 us -> none
where the time goes in v6:
time: 68.8 us; the launch traced here: 68.6 us
  Pallas kernels  64.3 us (93%)
  between operations  2.44 us (4%)
  other arithmetic  1.83 us (3%)
    pallas_call x1, Pallas kernels, local_part(): pl.pallas_call(kernel, out_shape=(jax.ShapeDtypeStruct((1, 1), jnp.float3...  64.3 us
    add x1, other arithmetic, local_part(): return (loss, near + far.astype(jnp.float32))  1.83 us

profile of v6, /device:TPU:57, one launch (start us, length us, event | category | flops | bytes accessed | tf_op | source)
XLA Modules:
  0.0 68.6 jit_solution(1114234453307253346)
XLA Ops:
  0.6 64.3 %shard_map.50 = (f32[1,1]{1,0:T(1,128)}, f32[128,768]{1,0:T(8,128)}, bf16[128,768]{1,0:T(8,128)(2,1)}) custom-call(bf16[128,768]{1,0:T(8,128)(2,1)} %student.1, bf16[128,768]{1,0:T(8,128)(2,1)} %teacher.1, s32[5]{0:T(128)} %codes.1), custom_call_target="tpu_custom_call" | custom-call | tf_op jit(solution)/shard_map/pallas_call | solution.py:532
  65.0 1.8 %convert_add_fusion = f32[128,768]{1,0:T(8,128)} fusion(f32[128,768]{1,0:T(8,128)} %get-tuple-element.6, bf16[128,768]{1,0:T(8,128)(2,1)} %get-tuple-element.7), kind=kLoop, calls=%fused_computation | loop fusion | flops 196608 | bytes 983040 | tf_op jit(solution)/shard_map/add | solution.py:579
